TPU v7x, 32 devices: a whole 2x2x4 slice. The times are simulated.
32 devices in a mesh: dp: 8 (over y, x, core), tensor: 4 (over z).
Axes of the slice: x: 2, y: 2, z: 4, core: 2. Of those that a mesh axis runs over, the one named last changes fastest.
Arguments:
- inputs: bfloat16 [2048, 1024], P(('dp', 'tensor')), may hold values from -6 to 6
- first_gain: float32 [1024], replicated, may hold values from 0.1 to 1.9
- entry_projection_weight: bfloat16 [3, 1024, 1024], P(None, 'dp', 'tensor'), may hold values from -0.1875 to 0.1875
- conv_weight: float32 [3, 1024], replicated, may hold values from -3 to 3
- out_weight: bfloat16 [1024, 1024], P('tensor', 'dp'), may hold values from -0.1875 to 0.1875
- second_gain: float32 [1024], replicated, may hold values from 0.1 to 1.9
- gate_up_weight: bfloat16 [2, 1024, 4608], P(None, 'dp', 'tensor'), may hold values from -0.1875 to 0.1875
- down_weight: bfloat16 [4608, 1024], P('tensor', 'dp'), may hold values from -0.09375 to 0.09375
- cotangent: bfloat16 [2048, 1024], P(('dp', 'tensor')), may hold values from -6 to 6
- lengths: int32 [4], replicated, may hold values from 1 to 1024, 2048 in all
Outputs:
- output: bfloat16 [2048, 1024], P(('dp', 'tensor'))
- input_grad: float32 [2048, 1024], P(('dp', 'tensor'))
- first_gain_grad: float32 [1024], replicated
- in_weight_grad: float32 [3, 1024, 1024], P(None, 'dp', 'tensor')
- filter_weight_gradient: float32 [3, 1024], replicated
- out_weight_grad: float32 [1024, 1024], P('tensor', 'dp')
- second_gain_grad: float32 [1024], replicated
- gate_up_grad: float32 [2, 1024, 4608], P(None, 'dp', 'tensor')
- down_grad: float32 [4608, 1024], P('tensor', 'dp')
Inputs may be any that keep to these rules, and one draw needn't show every extreme that they name: lengths of the 4 sequences packed end to end in token order; they sum to 2048, and the longest is exactly 1024.
All inputs are finite; a program needn't handle non-finite values.
Results may differ from a plain program's by a relative error of at most 0.012.
Values may be sent and summed in bfloat16 or wider, within the bound.
A program may use at most 128 MiB of HBM per device.

v0:
```python
import jax
import jax.numpy as jnp
from jax import lax
from jax.sharding import PartitionSpec as P

EPS = 1e-05


def passed_along(block, axis, distance):
    devices = range(lax.axis_size(axis))
    route = [(i - distance, i) for i in devices if i - distance in devices]
    return lax.ppermute(block, axis, route)


def rms_norm(values, gain):
    return values * lax.rsqrt(jnp.mean(values * values, axis=-1, keepdims=True) + EPS) * gain


def rms_back(values, gain, grad_out):
    scale = lax.rsqrt(jnp.mean(values * values, axis=-1, keepdims=True) + EPS)
    normal = values * scale
    weighted = gain * grad_out
    grad_in = scale * (weighted - normal * jnp.mean(normal * weighted, axis=-1, keepdims=True))
    return (grad_in, jnp.sum(normal * grad_out, axis=0))


def times_trans(left, right):
    return lax.dot_general(
        left, right, (((1,), (1,)), ((), ())), preferred_element_type=jnp.float32
    )


def trans_times(left, right):
    return lax.dot_general(
        left, right, (((0,), (0,)), ((), ())), preferred_element_type=jnp.float32
    )


def shards(
    inputs,
    first_gain,
    entry_projection_weight,
    conv_weight,
    out_weight,
    second_gain,
    gate_up_weight,
    down_weight,
    cotangent,
    lengths,
):
    own_rows = inputs.shape[0]
    group_rows = own_rows * lax.axis_size("tensor")
    channels = entry_projection_weight.shape[2]
    column = lax.axis_index("tensor") * channels
    start = lax.axis_index("dp") * group_rows
    ends = jnp.cumsum(lengths)
    places = start - 2 + jnp.arange(group_rows + 4, dtype=jnp.int32)
    segment = jnp.sum((places[:, None] >= ends[None, :]).astype(jnp.int32), axis=1)
    first_all = jnp.logical_and(segment[2:] == segment[1:-1], places[2:] >= 1).astype(jnp.float32)[
        :, None
    ]
    second_all = jnp.logical_and(segment[2:] == segment[:-2], places[2:] >= 2).astype(jnp.float32)[
        :, None
    ]
    first_keep = first_all[:group_rows]
    second_keep = second_all[:group_rows]
    kernel = lax.dynamic_slice_in_dim(conv_weight, column, channels, 1)
    residual = inputs.astype(jnp.float32)
    normed = lax.all_gather(
        rms_norm(residual, first_gain).astype(jnp.bfloat16), "tensor", axis=0, tiled=True
    )
    in_full, out_full, gate_up_full, down_full = (
        lax.all_gather(entry_projection_weight, "dp", axis=1, tiled=True),
        lax.all_gather(out_weight, "dp", axis=1, tiled=True),
        lax.all_gather(gate_up_weight, "dp", axis=1, tiled=True),
        lax.all_gather(down_weight, "dp", axis=1, tiled=True),
    )
    projected = jnp.einsum("td,kdc->ktc", normed, in_full, preferred_element_type=jnp.float32)
    input_gate_value = projected[0]
    c_value = projected[1]
    v_value = projected[2]
    product = (input_gate_value * v_value).astype(jnp.bfloat16)
    before = passed_along(product[-2:], "dp", 1)
    extended = jnp.concatenate([before, product], axis=0).astype(jnp.float32)
    mixed = (
        kernel[2] * extended[2:]
        + kernel[1] * first_keep * extended[1:-1]
        + kernel[0] * second_keep * extended[:-2]
    )
    gated = (c_value * mixed).astype(jnp.bfloat16)
    mixer_part = jnp.dot(gated, out_full, preferred_element_type=jnp.float32)
    middle = residual + lax.psum_scatter(mixer_part, "tensor", scatter_dimension=0, tiled=True)
    hidden_in = lax.all_gather(
        rms_norm(middle, second_gain).astype(jnp.bfloat16), "tensor", axis=0, tiled=True
    )
    gate_up = jnp.einsum("td,kdf->ktf", hidden_in, gate_up_full, preferred_element_type=jnp.float32)
    gate_value = gate_up[0]
    up_value = gate_up[1]
    sigmoid = jax.nn.sigmoid(gate_value)
    swish = gate_value * sigmoid
    hidden = (swish * up_value).astype(jnp.bfloat16)
    ffn_part = jnp.dot(hidden, down_full, preferred_element_type=jnp.float32)
    output = (
        middle
        + lax.psum_scatter(
            ffn_part.astype(jnp.bfloat16), "tensor", scatter_dimension=0, tiled=True
        ).astype(jnp.float32)
    ).astype(jnp.bfloat16)
    in_full, out_full, gate_up_full, down_full = (
        lax.all_gather(entry_projection_weight, "dp", axis=1, tiled=True),
        lax.all_gather(out_weight, "dp", axis=1, tiled=True),
        lax.all_gather(gate_up_weight, "dp", axis=1, tiled=True),
        lax.all_gather(down_weight, "dp", axis=1, tiled=True),
    )
    grad_rows = lax.all_gather(cotangent, "tensor", axis=0, tiled=True)
    grad_hidden = times_trans(grad_rows, down_full)
    down_part = trans_times(hidden, grad_rows)
    grad_gate = (grad_hidden * up_value * sigmoid * (1.0 + gate_value * (1.0 - sigmoid))).astype(
        jnp.bfloat16
    )
    grad_up = (grad_hidden * swish).astype(jnp.bfloat16)
    gate_up_stack = jnp.stack([grad_gate, grad_up])
    gate_up_part = jnp.einsum(
        "td,ktf->kdf", hidden_in, gate_up_stack, preferred_element_type=jnp.float32
    )
    hidden_back = jnp.einsum(
        "ktf,kdf->td", gate_up_stack, gate_up_full, preferred_element_type=jnp.float32
    )
    grad_hin = lax.psum_scatter(hidden_back, "tensor", scatter_dimension=0, tiled=True)
    second_back, second_part = rms_back(middle, second_gain, grad_hin)
    grad_middle = cotangent.astype(jnp.float32) + second_back
    branch_rows = lax.all_gather(grad_middle.astype(jnp.bfloat16), "tensor", axis=0, tiled=True)
    grad_gated = times_trans(branch_rows, out_full)
    out_part = trans_times(gated, branch_rows)
    output_gate_gradient = (grad_gated * mixed).astype(jnp.bfloat16)
    grad_mixed = (grad_gated * c_value).astype(jnp.bfloat16)
    after = passed_along(grad_mixed[:2], "dp", -1)
    grad_ext = jnp.concatenate([grad_mixed, after], axis=0).astype(jnp.float32)
    mixed_wide = grad_ext[:-2]
    kernel_part = jnp.stack(
        [
            jnp.sum(second_keep * extended[:-2] * mixed_wide, axis=0),
            jnp.sum(first_keep * extended[1:-1] * mixed_wide, axis=0),
            jnp.sum(extended[2:] * mixed_wide, axis=0),
        ]
    )
    kernel_full = lax.dynamic_update_slice_in_dim(
        jnp.zeros(conv_weight.shape, jnp.float32), kernel_part, column, 1
    )
    elementwise_product_gradient = (
        kernel[2] * grad_ext[:-2]
        + kernel[1] * first_all[1:-1] * grad_ext[1:-1]
        + kernel[0] * second_all[2:] * grad_ext[2:]
    )
    input_gate_gradient = (elementwise_product_gradient * v_value).astype(jnp.bfloat16)
    value_branch_gradient = (elementwise_product_gradient * input_gate_value).astype(jnp.bfloat16)
    stacked_projection_outputs = jnp.stack(
        [input_gate_gradient, output_gate_gradient, value_branch_gradient]
    )
    in_part = jnp.einsum(
        "td,ktc->kdc", normed, stacked_projection_outputs, preferred_element_type=jnp.float32
    )
    normed_back = jnp.einsum(
        "ktc,kdc->td", stacked_projection_outputs, in_full, preferred_element_type=jnp.float32
    )
    grad_normed = lax.psum_scatter(
        normed_back.astype(jnp.bfloat16), "tensor", scatter_dimension=0, tiled=True
    ).astype(jnp.float32)
    first_back, first_part = rms_back(residual, first_gain, grad_normed)
    input_grad = grad_middle + first_back
    in_grad, out_grad, gate_up_grad, down_grad = (
        lax.psum_scatter(in_part, "dp", scatter_dimension=1, tiled=True),
        lax.psum_scatter(out_part, "dp", scatter_dimension=1, tiled=True),
        lax.psum_scatter(gate_up_part, "dp", scatter_dimension=1, tiled=True),
        lax.psum_scatter(down_part, "dp", scatter_dimension=1, tiled=True),
    )
    first_gain_grad, second_gain_grad, conv_grad = lax.psum(
        (first_part, second_part, kernel_full), ("dp", "tensor")
    )
    return (
        output,
        input_grad,
        first_gain_grad,
        in_grad,
        conv_grad,
        out_grad,
        second_gain_grad,
        gate_up_grad,
        down_grad,
    )


def solution(mesh):
    in_specs = (
        P(("dp", "tensor"), None),
        P(),
        P(None, "dp", "tensor"),
        P(),
        P("tensor", "dp"),
        P(),
        P(None, "dp", "tensor"),
        P("tensor", "dp"),
        P(("dp", "tensor"), None),
        P(),
    )
    out_specs = (
        P(("dp", "tensor"), None),
        P(("dp", "tensor"), None),
        P(),
        P(None, "dp", "tensor"),
        P(),
        P("tensor", "dp"),
        P(),
        P(None, "dp", "tensor"),
        P("tensor", "dp"),
    )
    return jax.shard_map(shards, mesh=mesh, in_specs=in_specs, out_specs=out_specs, check_vma=False)
```

profile of v0, /device:TPU:0, one launch (start us, length us, event | category | flops | bytes accessed | tf_op | source)
XLA Modules:
  0.0 489.5 jit_solution(4341568830876603250)
XLA Ops:
  8.9 11.7 %all_gather.30 = bf16[256,1024]{1,0:T(8,128)(2,1)S(1)} all-gather(bf16[256,128]{1,0:T(8,128)(2,1)} %param.14), channel_id=1, replica_groups=mesh['dp'=8,'tensor'=4] {'dp'}, dimensions={1}, use_global_device_ids=true | all-gather | bytes 589824 | tf_op jit(solution)/shard_map/all_gather | solution.py:74
  22.8 16.4 %all_gather.28 = bf16[256,1024]{1,0:T(8,128)(2,1)S(1)} all-gather(bf16[64,1024]{1,0:T(8,128)(2,1)S(1)} %fusion.15), channel_id=1, replica_groups=mesh['dp'=8,'tensor'=4] {'tensor'}, dimensions={0}, use_global_device_ids=true | all-gather | bytes 655360 | tf_op jit(solution)/shard_map/all_gather | solution.py:69
  39.9 2.0 convolution_bitcast_fusion.5
  47.8 21.5 %all_gather.34 = bf16[256,1024]{1,0:T(8,128)(2,1)} all-gather(bf16[64,1024]{1,0:T(8,128)(2,1)S(1)} %copy-done.13), channel_id=1, replica_groups=mesh['dp'=8,'tensor'=4] {'tensor'}, dimensions={0}, use_global_device_ids=true | all-gather | bytes 655360 | tf_op jit(solution)/shard_map/all_gather | solution.py:115
  69.3 13.1 %reduce-scatter.9.cloned.1.call-done = f32[64,1024]{1,0:T(8,128)} async-done(((f32[256,1024]{1,0:T(8,128)}), f32[64,1024]{1,0:T(8,128)}) %reduce-scatter.9.cloned.1.call-update) | async-done | bytes 262160 | tf_op jit(solution)/shard_map/reduce_scatter | solution.py:92
  83.6 16.7 %all_gather.31 = bf16[256,1024]{1,0:T(8,128)(2,1)} all-gather(bf16[64,1024]{1,0:T(8,128)(2,1)S(1)} %multiply_convert_fusion.7), channel_id=1, replica_groups=mesh['dp'=8,'tensor'=4] {'tensor'}, dimensions={0}, use_global_device_ids=true | all-gather | bytes 655360 | tf_op jit(solution)/shard_map/all_gather | solution.py:93
  100.3 22.1 %all-gather.6.cloned.1.call-done = bf16[2,1024,1152]{2,1,0:T(8,128)(2,1)} async-done(((bf16[2,128,1152]{2,1,0:T(8,128)(2,1)}), bf16[2,1024,1152]{2,1,0:T(8,128)(2,1)}) %all-gather.6.cloned.1.call-update) | async-done | bytes 4718608 | tf_op jit(solution)/shard_map/all_gather | solution.py:75
  122.4 3.9 convolution_bitcast_fusion.1
  126.2 27.4 %all-gather.8.cloned.1.call-done = bf16[1152,1024]{1,0:T(8,128)(2,1)} async-done(((bf16[1152,128]{1,0:T(8,128)(2,1)}), bf16[1152,1024]{1,0:T(8,128)(2,1)}) %all-gather.8.cloned.1.call-update) | async-done | bytes 2359312 | tf_op jit(solution)/shard_map/all_gather | solution.py:76
  153.6 4.1 fusion.3
  158.7 2.4 convolution_bitcast_fusion.4
  161.2 27.2 %reduce-scatter.13.cloned.1.call-done = f32[64,1024]{1,0:T(8,128)} async-done(((f32[256,1024]{1,0:T(8,128)}), f32[64,1024]{1,0:T(8,128)}) %reduce-scatter.13.cloned.1.call-update) | async-done | bytes 262160 | tf_op jit(solution)/shard_map/reduce_scatter | solution.py:129
  191.3 15.9 %all_gather.35 = bf16[256,1024]{1,0:T(8,128)(2,1)S(1)} all-gather(bf16[64,1024]{1,0:T(8,128)(2,1)S(1)} %fusion.32), channel_id=1, replica_groups=mesh['dp'=8,'tensor'=4] {'tensor'}, dimensions={0}, use_global_device_ids=true | all-gather | bytes 655360 | tf_op jit(solution)/shard_map/all_gather | solution.py:132
  213.4 3.4 convolution_convert_fusion
  216.9 2.3 convolution_bitcast_fusion.2
  220.4 6.2 %convolution_bitcast_fusion = f32[2,1024,1152]{1,2,0:T(8,128)} fusion(bf16[1,256,1152]{2,1,0:T(8,128)(2,1)} %copy-done.20, bf16[1,256,1152]{2,1,0:T(8,128)(2,1)S(1)} %copy-done.19, bf16[256,1024]{1,0:T(8,128)(2,1)S(1)} %copy-done.3), kind=kOutput, calls=%fused_computation | convolution fusion | flops 1208549376 | bytes 11141120 | tf_op jit(solution)/shard_map/td,ktf->kdf/dot_general | solution.py:123
  228.8 3.0 fusion.40
  235.2 39.3 %all-reduce = (f32[1024]{0:T(1024)}, f32[3,1024]{1,0:T(4,128)}, f32[1024]{0:T(1024)}) all-reduce(f32[1024]{0:T(1024)S(1)} %get-tuple-element.32, f32[3,1024]{1,0:T(4,128)S(1)} %maximum_dynamic-update-slice_fusion, f32[1024]{0:T(1024)S(1)} %get-tuple-element.30), channel_id=1, replica_groups=mesh['dp'=8,'tensor'=4] {'dp','tensor'}, use_global_device_ids=true, to_apply=%region_11.12 | all-reduce | flops 5120 | bytes 40960 | tf_op jit(solution)/shard_map/psum | solution.py:177
  276.5 27.7 %reduce-scatter.17.cloned.1.call-done = f32[3,128,256]{1,2,0:T(8,128)} async-done(((f32[3,1024,256]{1,2,0:T(8,128)}), f32[3,128,256]{1,2,0:T(8,128)}) %reduce-scatter.17.cloned.1.call-update) | async-done | bytes 393232 | tf_op jit(solution)/shard_map/reduce_scatter | solution.py:172
  304.2 1.9 copy.25
  306.1 78.5 %reduce-scatter.21.cloned.1.call-done = f32[2,128,1152]{1,2,0:T(8,128)} async-done(((f32[2,1024,1152]{1,2,0:T(8,128)}), f32[2,128,1152]{1,2,0:T(8,128)}) %reduce-scatter.21.cloned.1.call-update) | async-done | bytes 1179664 | tf_op jit(solution)/shard_map/reduce_scatter | solution.py:174
  384.6 2.7 copy.26
  387.3 37.3 %reduce-scatter.19.cloned.1.call-done = f32[256,128]{1,0:T(8,128)} async-done(((f32[256,1024]{1,0:T(8,128)}), f32[256,128]{1,0:T(8,128)}) %reduce-scatter.19.cloned.1.call-update) | async-done | bytes 131088 | tf_op jit(solution)/shard_map/reduce_scatter | solution.py:173
  424.6 58.3 %reduce-scatter.23.cloned.1.call-done = f32[1152,128]{1,0:T(8,128)} async-done(((f32[1152,1024]{1,0:T(8,128)}), f32[1152,128]{1,0:T(8,128)}) %reduce-scatter.23.cloned.1.call-update) | async-done | bytes 589840 | tf_op jit(solution)/shard_map/reduce_scatter | solution.py:175
  (160 shorter events, 30.1 us)
Async XLA Ops:
  7.2 32.7 %all-gather.4.cloned.1.call-start = ((), (), s32[]{:S(2)}) async-start(), calls=%async_computation.8 | async-start | bytes 1769472 | tf_op jit(solution)/shard_map/all_gather | solution.py:73
  7.9 74.5 %reduce-scatter.9.cloned.1.call-start = ((), (), s32[]{:S(2)}) async-start(), calls=%async_computation.9 | async-start | bytes 1310720 | tf_op jit(solution)/shard_map/reduce_scatter | solution.py:92
  20.6 24.5 %copy-start.4 = (bf16[256,1024]{1,0:T(8,128)(2,1)}, bf16[256,1024]{1,0:T(8,128)(2,1)S(1)}, u32[]{:S(2)}) copy-start(bf16[256,1024]{1,0:T(8,128)(2,1)S(1)} %all_gather.30) | copy-start | bytes 1572868
  42.0 2.2 collective-permute-start
  46.4 36.0 %copy-start.8 = (bf16[64,1024]{1,0:T(8,128)(2,1)S(1)}, bf16[64,1024]{1,0:T(8,128)(2,1)}, u32[]{:S(2)}) copy-start(bf16[64,1024]{1,0:T(8,128)(2,1)} %param.10) | copy-start | bytes 393220
  46.4 37.1 %copy-start.25 = (f32[1024]{0:T(1024)S(1)}, f32[1024]{0:T(1024)}, u32[]{:S(2)}) copy-start(f32[1024]{0:T(1024)} %param.15) | copy-start | bytes 12292
  46.4 75.9 %all-gather.6.cloned.1.call-start = ((), (), s32[]{:S(2)}) async-start(), calls=%async_computation.10 | async-start | bytes 5308416 | tf_op jit(solution)/shard_map/all_gather | solution.py:75
  47.2 106.4 %all-gather.8.cloned.1.call-start = ((), (), s32[]{:S(2)}) async-start(), calls=%async_computation.11 | async-start | bytes 2654208 | tf_op jit(solution)/shard_map/all_gather | solution.py:76
  47.8 140.6 %reduce-scatter.13.cloned.1.call-start = ((), (), s32[]{:S(2)}) async-start(), calls=%async_computation.13 | async-start | bytes 1310720 | tf_op jit(solution)/shard_map/reduce_scatter | solution.py:129
  158.7 29.7 %copy-start.2 = (f32[64,1024]{1,0:T(8,128)S(1)}, f32[64,1024]{1,0:T(8,128)}, u32[]{:S(2)}) copy-start(f32[64,1024]{1,0:T(8,128)} %copy-done.1) | copy-start | bytes 786436
  158.7 29.7 %copy-start.38 = (f32[64]{0:T(128)S(1)}, f32[64]{0:T(128)}, u32[]{:S(2)}) copy-start(f32[64]{0:T(128)} %copy-done.37) | copy-start | bytes 772
  161.1 29.0 %copy-start.14 = (bf16[64,1024]{1,0:T(8,128)(2,1)S(1)}, bf16[64,1024]{1,0:T(8,128)(2,1)}, u32[]{:S(2)}) copy-start(bf16[64,1024]{1,0:T(8,128)(2,1)} %param.18) | copy-start | bytes 393220
  161.1 46.1 %copy-start.5 = (bf16[256,1024]{1,0:T(8,128)(2,1)S(1)}, bf16[256,1024]{1,0:T(8,128)(2,1)}, u32[]{:S(2)}) copy-start(bf16[256,1024]{1,0:T(8,128)(2,1)} %copy-done.4) | copy-start | bytes 1572868
  161.1 46.4 %copy-start.17 = (f32[256,256]{1,0:T(8,128)S(1)}, f32[256,256]{1,0:T(8,128)}, u32[]{:S(2)}) copy-start(f32[256,256]{1,0:T(8,128)} %get-tuple-element.42) | copy-start | bytes 786436
  161.1 73.0 %reduce-scatter.15.cloned.1.call-start = ((), (), s32[]{:S(2)}) async-start(), calls=%async_computation.14 | async-start | bytes 655360 | tf_op jit(solution)/shard_map/reduce_scatter | solution.py:166
  207.7 3.2 collective-permute-start.1
  213.3 61.3 %reduce-scatter.11.cloned.1.call-start = ((), (), s32[]{:S(2)}) async-start(), calls=%async_computation.12 | async-start | bytes 655360 | tf_op jit(solution)/shard_map/reduce_scatter | solution.py:105
  216.8 87.4 %reduce-scatter.17.cloned.1.call-start = ((), (), s32[]{:S(2)}) async-start(), calls=%async_computation.15 | async-start | bytes 3538944 | tf_op jit(solution)/shard_map/reduce_scatter | solution.py:172
  219.2 165.5 %reduce-scatter.21.cloned.1.call-start = ((), (), s32[]{:S(2)}) async-start(), calls=%async_computation.17 | async-start | bytes 10616832 | tf_op jit(solution)/shard_map/reduce_scatter | solution.py:174
  226.6 198.1 %reduce-scatter.19.cloned.1.call-start = ((), (), s32[]{:S(2)}) async-start(), calls=%async_computation.16 | async-start | bytes 1179648 | tf_op jit(solution)/shard_map/reduce_scatter | solution.py:173
  228.8 254.2 %reduce-scatter.23.cloned.1.call-start = ((), (), s32[]{:S(2)}) async-start(), calls=%async_computation.18 | async-start | bytes 5308416 | tf_op jit(solution)/shard_map/reduce_scatter | solution.py:175
  231.9 42.7 %copy-start.9 = (f32[64,1024]{1,0:T(8,128)S(1)}, f32[64,1024]{1,0:T(8,128)}, u32[]{:S(2)}) copy-start(f32[64,1024]{1,0:T(8,128)} %reduce-scatter.13.cloned.1.call-done) | copy-start | bytes 786436
  231.9 42.7 %copy-start.39 = (f32[64]{0:T(128)S(1)}, f32[64]{0:T(128)}, u32[]{:S(2)}) copy-start(f32[64]{0:T(128)} %copy-done.37) | copy-start | bytes 772
  231.9 42.7 %copy-start.48 = (f32[64]{0:T(128)S(1)}, f32[64]{0:T(128)}, u32[]{:S(2)}) copy-start(f32[64]{0:T(128)} %copy-done.47) | copy-start | bytes 772
  (38 other events, 248.9 us)
Sparse Core Ops, SparseCore 0:
  9.9 28.3 all-gather.3
  46.6 35.7 reduce-scatter.8
  84.4 37.8 all-gather.5
  124.2 29.3 all-gather.7
  161.2 27.1 reduce-scatter.12
  213.4 20.6 reduce-scatter.14
  236.4 19.9 reduce-scatter.10
  259.8 44.4 reduce-scatter.16
  308.1 76.4 reduce-scatter.20
  388.6 36.0 reduce-scatter.18
  429.0 53.8 reduce-scatter.22
where the time goes:
time: 490 us; the launch traced here: 489 us
  waiting for transfers between devices  297 us (61%)
  blocking collectives  121 us (25%)
  matrix products  31.5 us (6%)
  between operations  14.5 us (3%)
  other arithmetic  11.5 us (2%)
  local copies, waits for them, and re-layouts  10.4 us (2%)
    reduce_scatter x1, waiting for transfers between devices, shards(): lax.psum_scatter(gate_up_part, 'dp', scatter_dimension=1, tiled=True)  78.5 us
    reduce_scatter x1, waiting for transfers between devices, shards(): lax.psum_scatter(down_part, 'dp', scatter_dimension=1, tiled=True)  58.3 us
    psum x1, blocking collectives, shards(): lax.psum((first_part, second_part, kernel_full), ('dp', 'tensor'))  39.3 us
    reduce_scatter x1, waiting for transfers between devices, shards(): lax.psum_scatter(out_part, 'dp', scatter_dimension=1, tiled=True)  37.3 us
    reduce_scatter x1, waiting for transfers between devices, shards(): lax.psum_scatter(in_part, 'dp', scatter_dimension=1, tiled=True)  27.7 us
    all_gather x1, waiting for transfers between devices, shards(): lax.all_gather(down_weight, 'dp', axis=1, tiled=True)  27.4 us
    reduce_scatter x1, waiting for transfers between devices, shards(): lax.psum_scatter(hidden_back, 'tensor', scatter_dimension=0, tiled=True)  27.2 us
    all_gather x1, waiting for transfers between devices, shards(): lax.all_gather(gate_up_weight, 'dp', axis=1, tiled=True)  22.1 us
  transfers between devices with their start and end apart: 13, of which 10 were waited for; matrix products, arithmetic and copies ran while one was open for 7% of the time, Pallas kernels for 0%

commit v1 on v0

--- a/solution.py
+++ b/solution.py
@@ -4,6 +4,27 @@
 from jax.sharding import PartitionSpec as P
 
 EPS = 1e-05
+
+
+def gather_around(x, axis, dim):
+    count, index, span = (lax.axis_size(axis), lax.axis_index(axis), x.shape[dim])
+    right = [(i, (i + 1) % count) for i in range(count)]
+    left = [(i, (i - 1) % count) for i in range(count)]
+    out = jnp.zeros((*x.shape[:dim], count * span, *x.shape[dim + 1 :]), x.dtype)
+    out = lax.dynamic_update_slice_in_dim(out, x, index * span, axis=dim)
+    from_left = from_right = x
+    middle = count // 2
+    for step in range(1, middle + 1):
+        from_left = lax.ppermute(from_left, axis, right)
+        out = lax.dynamic_update_slice_in_dim(
+            out, from_left, (index - step) % count * span, axis=dim
+        )
+        if step < count - middle:
+            from_right = lax.ppermute(from_right, axis, left)
+            out = lax.dynamic_update_slice_in_dim(
+                out, from_right, (index + step) % count * span, axis=dim
+            )
+    return out
 
 
 def passed_along(block, axis, distance):
@@ -73,7 +94,7 @@
         lax.all_gather(entry_projection_weight, "dp", axis=1, tiled=True),
         lax.all_gather(out_weight, "dp", axis=1, tiled=True),
         lax.all_gather(gate_up_weight, "dp", axis=1, tiled=True),
-        lax.all_gather(down_weight, "dp", axis=1, tiled=True),
+        gather_around(down_weight, "dp", 1),
     )
     projected = jnp.einsum("td,kdc->ktc", normed, in_full, preferred_element_type=jnp.float32)
     input_gate_value = projected[0]

time: 490 us -> 490 us (level)
  waiting for transfers between devices: 297 us -> 276 us
  local copies, waits for them, and re-layouts: 10.4 us -> 22.3 us
  starting transfers between devices: 3.16 us -> 13.1 us
    reduce_scatter x1, waiting for transfers between devices: 27.2 us -> 5.17 us  [shards(): lax.psum_scatter(hidden_back, 'tensor', scatter_dimension=0, tiled=True)]
    ppermute x0 -> x7, waiting for transfers between devices: none -> 12.5 us  [the longest x4 12.5 us: gather_around(): from_left = lax.ppermute(from_left, axis, right)]
    dynamic_update_slice x0 -> x8, local copies, waits for them, and re-layouts: none -> 9.98 us  [the longest x4 5.02 us: gather_around(): lax.dynamic_update_slice_in_dim(out, from_left, (index - step) % count *...]
    ppermute x0 -> x7, starting transfers between devices: none -> 9.73 us  [the longest x3 7.66 us: gather_around(): from_right = lax.ppermute(from_right, axis, left)]
    reduce_scatter x1, waiting for transfers between devices: 27.7 us -> 20.1 us  [shards(): lax.psum_scatter(in_part, 'dp', scatter_dimension=1, tiled=True)]
  transfers between devices with their start and end apart: 13 -> 20, of which waited for: 10 -> 11; matrix products, arithmetic and copies ran while one was open for 7% -> 10% of each run, Pallas kernels for 0% -> 0%
where the time goes in v1:
time: 490 us
  waiting for transfers between devices  276 us (56%)
  blocking collectives  121 us (25%)
  matrix products  31.5 us (6%)
  local copies, waits for them, and re-layouts  22.3 us (5%)
  between operations  14.5 us (3%)
  starting transfers between devices  13.1 us (3%)
  other arithmetic  11.6 us (2%)
    reduce_scatter x1, waiting for transfers between devices, shards(): lax.psum_scatter(gate_up_part, 'dp', scatter_dimension=1, tiled=True)  78.5 us
    reduce_scatter x1, waiting for transfers between devices, shards(): lax.psum_scatter(down_part, 'dp', scatter_dimension=1, tiled=True)  58.3 us
    psum x1, blocking collectives, shards(): lax.psum((first_part, second_part, kernel_full), ('dp', 'tensor'))  38.4 us
    reduce_scatter x1, waiting for transfers between devices, shards(): lax.psum_scatter(out_part, 'dp', scatter_dimension=1, tiled=True)  37.4 us
    all_gather x1, waiting for transfers between devices, shards(): lax.all_gather(down_weight, 'dp', axis=1, tiled=True)  27.4 us
    all_gather x1, blocking collectives, shards(): grad_rows = lax.all_gather(cotangent, 'tensor', axis=0, tiled=True)  21.6 us
    all_gather x1, waiting for transfers between devices, shards(): lax.all_gather(gate_up_weight, 'dp', axis=1, tiled=True)  21.4 us
    reduce_scatter x1, waiting for transfers between devices, shards(): lax.psum_scatter(in_part, 'dp', scatter_dimension=1, tiled=True)  20.1 us
  transfers between devices with their start and end apart: 20, of which 11 were waited for; matrix products, arithmetic and copies ran while one was open for 10% of the time, Pallas kernels for 0%

profile of v1, /device:TPU:0, one launch (start us, length us, event | category | flops | bytes accessed | tf_op | source)
XLA Modules:
  0.0 489.6 jit_solution(7393284943011213073)
XLA Ops:
  8.9 11.7 %all_gather.29 = bf16[256,1024]{1,0:T(8,128)(2,1)S(1)} all-gather(bf16[256,128]{1,0:T(8,128)(2,1)} %param.14), channel_id=1, replica_groups=mesh['dp'=8,'tensor'=4] {'dp'}, dimensions={1}, use_global_device_ids=true | all-gather | bytes 589824 | tf_op jit(solution)/shard_map/all_gather | solution.py:95
  22.8 16.4 %all_gather.27 = bf16[256,1024]{1,0:T(8,128)(2,1)S(1)} all-gather(bf16[64,1024]{1,0:T(8,128)(2,1)S(1)} %fusion.15), channel_id=1, replica_groups=mesh['dp'=8,'tensor'=4] {'tensor'}, dimensions={0}, use_global_device_ids=true | all-gather | bytes 655360 | tf_op jit(solution)/shard_map/all_gather | solution.py:90
  47.8 21.6 %all_gather.32 = bf16[256,1024]{1,0:T(8,128)(2,1)} all-gather(bf16[64,1024]{1,0:T(8,128)(2,1)S(1)} %copy-done.14), channel_id=1, replica_groups=mesh['dp'=8,'tensor'=4] {'tensor'}, dimensions={0}, use_global_device_ids=true | all-gather | bytes 655360 | tf_op jit(solution)/shard_map/all_gather | solution.py:136
  69.4 13.0 %reduce-scatter.9.cloned.1.call-done = f32[64,1024]{1,0:T(8,128)} async-done(((f32[256,1024]{1,0:T(8,128)}), f32[64,1024]{1,0:T(8,128)}) %reduce-scatter.9.cloned.1.call-update) | async-done | bytes 262160 | tf_op jit(solution)/shard_map/reduce_scatter | solution.py:113
  84.3 16.7 %all_gather.30 = bf16[256,1024]{1,0:T(8,128)(2,1)} all-gather(bf16[64,1024]{1,0:T(8,128)(2,1)S(1)} %multiply_convert_fusion.7), channel_id=1, replica_groups=mesh['dp'=8,'tensor'=4] {'tensor'}, dimensions={0}, use_global_device_ids=true | all-gather | bytes 655360 | tf_op jit(solution)/shard_map/all_gather | solution.py:114
  101.0 21.4 %all-gather.6.cloned.1.call-done = bf16[2,1024,1152]{2,1,0:T(8,128)(2,1)} async-done(((bf16[2,128,1152]{2,1,0:T(8,128)(2,1)}), bf16[2,1024,1152]{2,1,0:T(8,128)(2,1)}) %all-gather.6.cloned.1.call-update) | async-done | bytes 4718608 | tf_op jit(solution)/shard_map/all_gather | solution.py:96
  122.4 3.9 convolution_bitcast_fusion.1
  126.3 27.4 %all-gather.8.cloned.1.call-done = bf16[1152,1024]{1,0:T(8,128)(2,1)} async-done(((bf16[1152,128]{1,0:T(8,128)(2,1)}), bf16[1152,1024]{1,0:T(8,128)(2,1)}) %all-gather.8.cloned.1.call-update) | async-done | bytes 2359312 | tf_op jit(solution)/shard_map/all_gather | solution.py:134
  153.6 4.1 fusion.3
  166.5 4.2 collective-permute-done.1
  170.7 2.6 collective-permute-start.4
  174.9 5.8 %collective-permute-done.3 = bf16[1152,128]{1,0:T(8,128)(2,1)} collective-permute-done((bf16[1152,128]{1,0:T(8,128)(2,1)S(1)}, bf16[1152,128]{1,0:T(8,128)(2,1)}, u32[]{:S(2)}, u32[]{:S(2)}) %collective-permute-start.3) | collective-permute-done | bytes 294944 | tf_op jit(solution)/shard_map/ppermute | solution.py:18
  180.6 2.6 collective-permute-start.6
  183.3 5.2 %reduce-scatter.13.cloned.1.call-done = f32[64,1024]{1,0:T(8,128)} async-done(((f32[256,1024]{1,0:T(8,128)}), f32[64,1024]{1,0:T(8,128)}) %reduce-scatter.13.cloned.1.call-update) | async-done | bytes 262160 | tf_op jit(solution)/shard_map/reduce_scatter | solution.py:150
  190.9 16.1 %all_gather.34 = bf16[256,1024]{1,0:T(8,128)(2,1)S(1)} all-gather(bf16[64,1024]{1,0:T(8,128)(2,1)S(1)} %fusion.32), channel_id=1, replica_groups=mesh['dp'=8,'tensor'=4] {'tensor'}, dimensions={0}, use_global_device_ids=true | all-gather | bytes 655360 | tf_op jit(solution)/shard_map/all_gather | solution.py:153
  223.3 3.4 convolution_convert_fusion
  230.3 6.1 %convolution_bitcast_fusion = f32[2,1024,1152]{1,2,0:T(8,128)} fusion(bf16[1,256,1152]{2,1,0:T(8,128)(2,1)} %copy-done.21, bf16[1,256,1152]{2,1,0:T(8,128)(2,1)S(1)} %copy-done.20, bf16[256,1024]{1,0:T(8,128)(2,1)S(1)} %copy-done.3), kind=kOutput, calls=%fused_computation | convolution fusion | flops 1208549376 | bytes 11141120 | tf_op jit(solution)/shard_map/td,ktf->kdf/dot_general | solution.py:144
  238.9 3.0 fusion.40
  243.8 38.4 %all-reduce = (f32[1024]{0:T(1024)}, f32[3,1024]{1,0:T(4,128)}, f32[1024]{0:T(1024)}) all-reduce(f32[1024]{0:T(1024)S(1)} %get-tuple-element.32, f32[3,1024]{1,0:T(4,128)S(1)} %maximum_dynamic-update-slice_fusion, f32[1024]{0:T(1024)S(1)} %get-tuple-element.30), channel_id=1, replica_groups=mesh['dp'=8,'tensor'=4] {'dp','tensor'}, use_global_device_ids=true, to_apply=%region_11.12 | all-reduce | flops 5120 | bytes 40960 | tf_op jit(solution)/shard_map/psum | solution.py:198
  284.2 20.1 %reduce-scatter.17.cloned.1.call-done = f32[3,128,256]{1,2,0:T(8,128)} async-done(((f32[3,1024,256]{1,2,0:T(8,128)}), f32[3,128,256]{1,2,0:T(8,128)}) %reduce-scatter.17.cloned.1.call-update) | async-done | bytes 393232 | tf_op jit(solution)/shard_map/reduce_scatter | solution.py:193
  306.2 78.5 %reduce-scatter.21.cloned.1.call-done = f32[2,128,1152]{1,2,0:T(8,128)} async-done(((f32[2,1024,1152]{1,2,0:T(8,128)}), f32[2,128,1152]{1,2,0:T(8,128)}) %reduce-scatter.21.cloned.1.call-update) | async-done | bytes 1179664 | tf_op jit(solution)/shard_map/reduce_scatter | solution.py:195
  384.7 2.7 copy.26
  387.4 37.4 %reduce-scatter.19.cloned.1.call-done = f32[256,128]{1,0:T(8,128)} async-done(((f32[256,1024]{1,0:T(8,128)}), f32[256,128]{1,0:T(8,128)}) %reduce-scatter.19.cloned.1.call-update) | async-done | bytes 131088 | tf_op jit(solution)/shard_map/reduce_scatter | solution.py:194
  424.7 58.3 %reduce-scatter.23.cloned.1.call-done = f32[1152,128]{1,0:T(8,128)} async-done(((f32[1152,1024]{1,0:T(8,128)}), f32[1152,128]{1,0:T(8,128)}) %reduce-scatter.23.cloned.1.call-update) | async-done | bytes 589840 | tf_op jit(solution)/shard_map/reduce_scatter | solution.py:196
  (185 shorter events, 54.6 us)
Async XLA Ops:
  7.2 32.7 %all-gather.4.cloned.1.call-start = ((), (), s32[]{:S(2)}) async-start(), calls=%async_computation.8 | async-start | bytes 1769472 | tf_op jit(solution)/shard_map/all_gather | solution.py:94
  7.9 74.5 %reduce-scatter.9.cloned.1.call-start = ((), (), s32[]{:S(2)}) async-start(), calls=%async_computation.9 | async-start | bytes 1310720 | tf_op jit(solution)/shard_map/reduce_scatter | solution.py:113
  42.0 2.2 collective-permute-start
  46.4 75.9 %all-gather.6.cloned.1.call-start = ((), (), s32[]{:S(2)}) async-start(), calls=%async_computation.10 | async-start | bytes 5308416 | tf_op jit(solution)/shard_map/all_gather | solution.py:96
  47.2 106.4 %all-gather.8.cloned.1.call-start = ((), (), s32[]{:S(2)}) async-start(), calls=%async_computation.12 | async-start | bytes 2654208 | tf_op jit(solution)/shard_map/all_gather | solution.py:134
  47.8 140.7 %reduce-scatter.13.cloned.1.call-start = ((), (), s32[]{:S(2)}) async-start(), calls=%async_computation.13 | async-start | bytes 1310720 | tf_op jit(solution)/shard_map/reduce_scatter | solution.py:150
  161.2 81.5 %reduce-scatter.15.cloned.1.call-start = ((), (), s32[]{:S(2)}) async-start(), calls=%async_computation.14 | async-start | bytes 655360 | tf_op jit(solution)/shard_map/reduce_scatter | solution.py:187
  161.2 9.4 %collective-permute-start.1 = (bf16[1152,128]{1,0:T(8,128)(2,1)S(1)}, bf16[1152,128]{1,0:T(8,128)(2,1)S(1)}, u32[]{:S(2)}, u32[]{:S(2)}) collective-permute-start(bf16[1152,128]{1,0:T(8,128)(2,1)S(1)} %copy-done.13), channel_id=1, source_target_pairs={{0,4},{4,8},{8,12},{12,16},{16,20},{20,24},{24,28},{28,0},{1,5},{5... | collective-permute-start | bytes 884744 | tf_op jit(solution)/shard_map/ppermute | solution.py:18
  161.6 9.1 %collective-permute-start.2 = (bf16[1152,128]{1,0:T(8,128)(2,1)S(1)}, bf16[1152,128]{1,0:T(8,128)(2,1)S(1)}, u32[]{:S(2)}, u32[]{:S(2)}) collective-permute-start(bf16[1152,128]{1,0:T(8,128)(2,1)S(1)} %copy-done.13), channel_id=1, source_target_pairs={{0,28},{4,0},{8,4},{12,8},{16,12},{20,16},{24,20},{28,24},{1,29},{... | collective-permute-start | bytes 884744 | tf_op jit(solution)/shard_map/ppermute | solution.py:23
  165.7 41.2 %copy-start.5 = (bf16[256,1024]{1,0:T(8,128)(2,1)S(1)}, bf16[256,1024]{1,0:T(8,128)(2,1)}, u32[]{:S(2)}) copy-start(bf16[256,1024]{1,0:T(8,128)(2,1)} %copy-done.4) | copy-start | bytes 1572868
  166.5 40.8 %copy-start.18 = (f32[256,256]{1,0:T(8,128)S(1)}, f32[256,256]{1,0:T(8,128)}, u32[]{:S(2)}) copy-start(f32[256,256]{1,0:T(8,128)} %get-tuple-element.42) | copy-start | bytes 786436
  170.7 10.0 %collective-permute-start.3 = (bf16[1152,128]{1,0:T(8,128)(2,1)S(1)}, bf16[1152,128]{1,0:T(8,128)(2,1)}, u32[]{:S(2)}, u32[]{:S(2)}) collective-permute-start(bf16[1152,128]{1,0:T(8,128)(2,1)S(1)} %collective-permute-done.1), channel_id=1, source_target_pairs={{0,4},{4,8},{8,12},{12,16},{16,20},{20,24},{24,28},{28,0},{1,5},{5... | collective-permute-start | bytes 884744 | tf_op jit(solution)/shard_map/ppermute | solution.py:18
  170.7 10.0 %collective-permute-start.4 = (bf16[1152,128]{1,0:T(8,128)(2,1)S(1)}, bf16[1152,128]{1,0:T(8,128)(2,1)}, u32[]{:S(2)}, u32[]{:S(2)}) collective-permute-start(bf16[1152,128]{1,0:T(8,128)(2,1)S(1)} %collective-permute-done.2), channel_id=1, source_target_pairs={{0,28},{4,0},{8,4},{12,8},{16,12},{20,16},{24,20},{28,24},{1,29},{... | collective-permute-start | bytes 884744 | tf_op jit(solution)/shard_map/ppermute | solution.py:23
  180.6 34.1 %collective-permute-start.5 = (bf16[1152,128]{1,0:T(8,128)(2,1)}, bf16[1152,128]{1,0:T(8,128)(2,1)}, u32[]{:S(2)}, u32[]{:S(2)}) collective-permute-start(bf16[1152,128]{1,0:T(8,128)(2,1)} %collective-permute-done.3), channel_id=1, source_target_pairs={{0,4},{4,8},{8,12},{12,16},{16,20},{20,24},{24,28},{28,0},{1,5},{5... | collective-permute-start | bytes 884744 | tf_op jit(solution)/shard_map/ppermute | solution.py:18
  180.6 37.6 %collective-permute-start.6 = (bf16[1152,128]{1,0:T(8,128)(2,1)}, bf16[1152,128]{1,0:T(8,128)(2,1)}, u32[]{:S(2)}, u32[]{:S(2)}) collective-permute-start(bf16[1152,128]{1,0:T(8,128)(2,1)} %collective-permute-done.4), channel_id=1, source_target_pairs={{0,28},{4,0},{8,4},{12,8},{16,12},{20,16},{24,20},{28,24},{1,29},{... | collective-permute-start | bytes 884744 | tf_op jit(solution)/shard_map/ppermute | solution.py:23
  207.4 3.2 collective-permute-start.8
  213.0 69.3 %reduce-scatter.11.cloned.1.call-start = ((), (), s32[]{:S(2)}) async-start(), calls=%async_computation.11 | async-start | bytes 655360 | tf_op jit(solution)/shard_map/reduce_scatter | solution.py:126
  214.8 7.7 %collective-permute-start.7 = (bf16[1152,128]{1,0:T(8,128)(2,1)}, bf16[1152,128]{1,0:T(8,128)(2,1)S(1)}, u32[]{:S(2)}, u32[]{:S(2)}) collective-permute-start(bf16[1152,128]{1,0:T(8,128)(2,1)} %collective-permute-done.5), channel_id=1, source_target_pairs={{0,4},{4,8},{8,12},{12,16},{16,20},{20,24},{24,28},{28,0},{1,5},{5... | collective-permute-start | bytes 884744 | tf_op jit(solution)/shard_map/ppermute | solution.py:18
  226.7 77.6 %reduce-scatter.17.cloned.1.call-start = ((), (), s32[]{:S(2)}) async-start(), calls=%async_computation.15 | async-start | bytes 3538944 | tf_op jit(solution)/shard_map/reduce_scatter | solution.py:193
  229.1 155.6 %reduce-scatter.21.cloned.1.call-start = ((), (), s32[]{:S(2)}) async-start(), calls=%async_computation.17 | async-start | bytes 10616832 | tf_op jit(solution)/shard_map/reduce_scatter | solution.py:195
  236.5 188.3 %reduce-scatter.19.cloned.1.call-start = ((), (), s32[]{:S(2)}) async-start(), calls=%async_computation.16 | async-start | bytes 1179648 | tf_op jit(solution)/shard_map/reduce_scatter | solution.py:194
  238.7 244.4 %reduce-scatter.23.cloned.1.call-start = ((), (), s32[]{:S(2)}) async-start(), calls=%async_computation.18 | async-start | bytes 5308416 | tf_op jit(solution)/shard_map/reduce_scatter | solution.py:196
  241.9 40.3 %copy-start.9 = (f32[64,1024]{1,0:T(8,128)S(1)}, f32[64,1024]{1,0:T(8,128)}, u32[]{:S(2)}) copy-start(f32[64,1024]{1,0:T(8,128)} %reduce-scatter.13.cloned.1.call-done) | copy-start | bytes 786436
  241.9 40.3 %copy-start.40 = (f32[64]{0:T(128)S(1)}, f32[64]{0:T(128)}, u32[]{:S(2)}) copy-start(f32[64]{0:T(128)} %copy-done.38) | copy-start | bytes 772
  (46 other events, 532.5 us)
Sparse Core Ops, SparseCore 0:
  9.9 28.3 all-gather.3
  46.6 35.7 reduce-scatter.8
  84.5 37.8 all-gather.5
  124.3 29.3 all-gather.7
  161.3 27.1 reduce-scatter.12
  213.1 20.7 reduce-scatter.14
  236.1 19.9 reduce-scatter.10
  259.5 44.7 reduce-scatter.16
  308.2 76.4 reduce-scatter.20
  388.6 36.0 reduce-scatter.18
  429.1 53.8 reduce-scatter.22
